TPU v7x, 256 devices: a whole 4x4x8 slice. The times are simulated.
256 devices in a mesh: grp: 8 (over z), dom: 32 (over x, y, core).
Axes of the slice: x: 4, y: 4, z: 8, core: 2. Of those that a mesh axis runs over, the one named last changes fastest.
Arguments:
- right_side: float32 [8, 32, 5, 2048], P('grp', 'dom'), may hold values from -6 to 6
- initial_guess: float32 [8, 32, 5, 2048], P('grp', 'dom'), may hold values from -3 to 3
- fine_diag: float32 [8, 32, 5, 5, 2048], P('grp', 'dom')
- fine_inverse: float32 [8, 32, 5, 5, 2048], P('grp', 'dom')
- fine_coupling: float32 [8, 32, 6, 5, 5, 2048], P('grp', 'dom'), may hold values from -1.4 to 1.4
- fine_columns: int32 [8, 32, 6, 2048], P('grp', 'dom'), may hold values from 0 to 2303, as said below
- fine_send: int32 [8, 32, 4, 64], P('grp', 'dom'), may hold values from 0 to 2047
- fine_count: int32 [8, 32, 4], P('grp', 'dom'), may hold values from 16 to 64, as said below
- fine_aggregate: int32 [8, 32, 2048], P('grp', 'dom'), may hold values from 0 to 511, as said below
- middle_diag: float32 [8, 32, 5, 5, 512], P('grp', 'dom')
- middle_inverse: float32 [8, 32, 5, 5, 512], P('grp', 'dom')
- middle_coupling: float32 [8, 32, 6, 5, 5, 512], P('grp', 'dom'), may hold values from -1.4 to 1.4
- middle_columns: int32 [8, 32, 6, 512], P('grp', 'dom'), may hold values from 0 to 1087
- middle_aggregate: int32 [8, 32, 512], P('grp', 'dom'), may hold values from 0 to 127, as said below
- coarse_diag: float32 [8, 32, 5, 5, 128], P('grp', 'dom')
- coarse_inverse: float32 [8, 32, 5, 5, 128], P('grp', 'dom')
- coarse_coupling: float32 [8, 32, 6, 5, 5, 128], P('grp', 'dom'), may hold values from -1.4 to 1.4
- coarse_columns: int32 [8, 32, 6, 128], P('grp', 'dom'), may hold values from 0 to 511
Outputs:
- solution: float32 [8, 32, 5, 2048], P('grp', 'dom')
Inputs may be any that keep to these rules, and one draw needn't show every extreme that they name: `fine_count`: at least one of the four counts of each device is 64; the others are ragged. `fine_columns`: columns below 2048 are own rows; a column 2048 + j * 64 + s names slot s of the j-th received block, with s below the sender's count. `fine_aggregate`: each middle row gathers exactly four fine rows of its device. `middle_aggregate`: each coarse row gathers exactly four middle rows of its device.
All inputs are finite; a program needn't handle non-finite values.
Results may differ from a plain program's by a relative error of at most 0.0003.
Values sent between devices are 32-bit elements; how exact they have to be, the bound alone decides.
No kernel may reach another device: no remote copies, remote signals or barrier semaphores. Data moves between devices by JAX's collectives and lax.ppermute only.
A program may use at most 128 MiB of HBM per device.

v0:
```python
import jax
import jax.numpy as jnp
from jax import lax
from jax.sharding import PartitionSpec as P

ROWS_MID = 512
ROWS_COARSE = 128
RIM_ROWS = 32
SWEEPS_FINE = 2
SWEEPS_MID = 2
SWEEPS_COARSE = 3


OFFSETS = (-2, -1, 1, 2)
relaxation = 0.8


def passed_along(x, axis, by):
    size = lax.axis_size(axis)
    return lax.ppermute(x, axis, [(i, (i + by) % size) for i in range(size)])


def with_halo(block, sides, width):
    for axis, dim in sides:
        count = lax.axis_size(axis)
        forward = [(i, i + 1) for i in range(count - 1)]
        forward.append((count - 1, 0))
        backward = [(target, source) for source, target in forward]
        low = lax.ppermute(
            lax.slice_in_dim(block, block.shape[dim] - width, None, axis=dim), axis, forward
        )
        high = lax.ppermute(lax.slice_in_dim(block, 0, width, axis=dim), axis, backward)
        block = jnp.concatenate([low, block, high], axis=dim)
    return block


def partner_2(x, axis, distance):
    return lax.ppermute(x, axis, [(i, i ^ 1 << distance) for i in range(lax.axis_size(axis))])


def block_product(blocks, vectors):
    total = blocks[:, 0] * vectors[0]
    for inner in range(1, blocks.shape[1]):
        total = total + blocks[:, inner] * vectors[inner]
    return total


def apply_rows(diag, coupling, columns, field, extended):
    image = block_product(diag, field)
    for neighbor in range(columns.shape[0]):
        picked = jnp.take(extended, columns[neighbor], axis=1)
        image = image + block_product(coupling[neighbor], picked)
    return image


def sweep_rows(diag, inverse, coupling, columns, field, target, extended):
    image = apply_rows(diag, coupling, columns, field, extended)
    return field + relaxation * block_product(inverse, target - image)


def residual_rows(diag, coupling, columns, field, target, extended):
    return target - apply_rows(diag, coupling, columns, field, extended)


def restrict_rows(residual, aggregate, number):
    return jax.ops.segment_sum(residual.T, aggregate, num_segments=number).T


def prolong_rows(correction, aggregate):
    return jnp.take(correction, aggregate, axis=1)


def fine_extend(field, send, count):
    slot_rows = send.shape[-1]
    positions = jnp.arange(slot_rows)
    slots = [
        jnp.take(field, send[peer_slot], axis=1)
        * (positions < count[peer_slot]).astype(jnp.float32)[None, :]
        for peer_slot in range(4)
    ]
    blocks = [
        passed_along(slots[3 - position], "dom", -offset) for position, offset in enumerate(OFFSETS)
    ]
    return jnp.concatenate([field] + blocks, axis=-1)


def middle_extend(field):
    rimmed = with_halo(field, (("dom", 1),), RIM_ROWS)
    partner = partner_2(field, "grp", 0)
    return jnp.concatenate([rimmed, partner], axis=-1)


def coarse_extend(field):
    members = field
    for bit_number in (0, 1):
        members = jnp.concatenate([members, partner_2(members, "grp", bit_number)], axis=-1)
    return members


def per_device(
    right_side,
    initial_guess,
    fine_diag,
    fine_inverse,
    fine_coupling,
    fine_columns,
    fine_send,
    fine_count,
    fine_aggregate,
    middle_diag,
    middle_inverse,
    middle_coupling,
    middle_columns,
    middle_aggregate,
    coarse_diag,
    coarse_inverse,
    coarse_coupling,
    coarse_columns,
):
    target = right_side[0, 0]
    f_diag, f_inverse, f_coupling, f_columns = (
        fine_diag[0, 0],
        fine_inverse[0, 0],
        fine_coupling[0, 0],
        fine_columns[0, 0],
    )
    f_send, f_count, f_aggregate = (fine_send[0, 0], fine_count[0, 0], fine_aggregate[0, 0])
    m_diag, m_inverse, m_coupling, m_columns = (
        middle_diag[0, 0],
        middle_inverse[0, 0],
        middle_coupling[0, 0],
        middle_columns[0, 0],
    )
    m_aggregate = middle_aggregate[0, 0]
    c_diag, c_inverse, c_coupling, c_columns = (
        coarse_diag[0, 0],
        coarse_inverse[0, 0],
        coarse_coupling[0, 0],
        coarse_columns[0, 0],
    )

    def fine_sweep(field):
        return sweep_rows(
            f_diag,
            f_inverse,
            f_coupling,
            f_columns,
            field,
            target,
            fine_extend(field, f_send, f_count),
        )

    def middle_sweep(field, goal):
        return sweep_rows(
            m_diag, m_inverse, m_coupling, m_columns, field, goal, middle_extend(field)
        )

    field = initial_guess[0, 0]
    for step in range(SWEEPS_FINE):
        field = fine_sweep(field)
    fine_residual = residual_rows(
        f_diag, f_coupling, f_columns, field, target, fine_extend(field, f_send, f_count)
    )
    middle_rhs = restrict_rows(fine_residual, f_aggregate, ROWS_MID)
    middle_field = jnp.zeros_like(middle_rhs)
    for step in range(SWEEPS_MID):
        middle_field = middle_sweep(middle_field, middle_rhs)
    middle_residual = residual_rows(
        m_diag, m_coupling, m_columns, middle_field, middle_rhs, middle_extend(middle_field)
    )
    coarse_rhs = restrict_rows(middle_residual, m_aggregate, ROWS_COARSE)
    coarse_field = jnp.zeros_like(coarse_rhs)
    for step in range(SWEEPS_COARSE):
        coarse_field = sweep_rows(
            c_diag,
            c_inverse,
            c_coupling,
            c_columns,
            coarse_field,
            coarse_rhs,
            coarse_extend(coarse_field),
        )
    middle_field = middle_field + prolong_rows(coarse_field, m_aggregate)
    for step in range(SWEEPS_MID):
        middle_field = middle_sweep(middle_field, middle_rhs)
    field = field + prolong_rows(middle_field, f_aggregate)
    for step in range(SWEEPS_FINE):
        field = fine_sweep(field)
    return field[None, None]


def solution(mesh):
    return jax.shard_map(
        per_device,
        mesh=mesh,
        in_specs=(
            P("grp", "dom", None, None),
            P("grp", "dom", None, None),
            P("grp", "dom", None, None, None),
            P("grp", "dom", None, None, None),
            P("grp", "dom", None, None, None, None),
            P("grp", "dom", None, None),
            P("grp", "dom", None, None),
            P("grp", "dom", None),
            P("grp", "dom", None),
            P("grp", "dom", None, None, None),
            P("grp", "dom", None, None, None),
            P("grp", "dom", None, None, None, None),
            P("grp", "dom", None, None),
            P("grp", "dom", None),
            P("grp", "dom", None, None, None),
            P("grp", "dom", None, None, None),
            P("grp", "dom", None, None, None, None),
            P("grp", "dom", None, None),
        ),
        out_specs=P("grp", "dom", None, None),
        check_vma=False,
    )
```

profile of v0, /device:TPU:1, one launch (start us, length us, event | category | flops | bytes accessed | tf_op | source)
XLA Modules:
  0.0 838.4 jit_solution(4090588465438327989)
XLA Ops:
  82.6 9.0 %gather_fusion.6 = f32[2048,5]{1,0:T(8,128)} fusion(f32[5,2304]{0,1:T(8,128)} %copy.610, s32[2048]{0:T(1024)S(1)} %copy-done.145), kind=kCustom, calls=%fused_computation.1.clone | custom fusion | bytes 90112 | tf_op jit(solution)/shard_map/jit(_take)/gather | solution.py:51
  96.2 8.8 %gather_fusion.7 = f32[2048,5]{1,0:T(8,128)} fusion(f32[5,2304]{0,1:T(8,128)} %copy.610, s32[2048]{0:T(1024)S(1)} %copy-done.147), kind=kCustom, calls=%fused_computation.23.clone | custom fusion | bytes 90112 | tf_op jit(solution)/shard_map/jit(_take)/gather | solution.py:51
  109.8 8.8 %gather_fusion.8 = f32[2048,5]{1,0:T(8,128)} fusion(f32[5,2304]{0,1:T(8,128)} %copy.610, s32[2048]{0:T(1024)S(1)} %copy-done.149), kind=kCustom, calls=%fused_computation.24.clone | custom fusion | bytes 90112 | tf_op jit(solution)/shard_map/jit(_take)/gather | solution.py:51
  123.3 8.8 %gather_fusion.9 = f32[2048,5]{1,0:T(8,128)} fusion(f32[5,2304]{0,1:T(8,128)} %copy.610, s32[2048]{0:T(1024)S(1)} %copy-done.152), kind=kCustom, calls=%fused_computation.25.clone | custom fusion | bytes 90112 | tf_op jit(solution)/shard_map/jit(_take)/gather | solution.py:51
  136.8 9.7 %gather_fusion.10 = f32[2048,5]{1,0:T(8,128)} fusion(f32[5,2304]{0,1:T(8,128)} %copy.610, s32[2048]{0:T(1024)} %fusion.227), kind=kCustom, calls=%fused_computation.26.clone | custom fusion | bytes 90112 | tf_op jit(solution)/shard_map/jit(_take)/gather | solution.py:51
  151.2 9.5 %gather_fusion.11 = f32[2048,5]{1,0:T(8,128)} fusion(f32[5,2304]{0,1:T(8,128)} %copy.610, s32[2048]{0:T(1024)} %fusion.228), kind=kCustom, calls=%fused_computation.27.clone | custom fusion | bytes 90112 | tf_op jit(solution)/shard_map/jit(_take)/gather | solution.py:51
  201.8 8.8 %gather_fusion.16 = f32[2048,5]{1,0:T(8,128)} fusion(f32[5,2304]{0,1:T(8,128)} %copy.636, s32[2048]{0:T(1024)S(1)} %copy-done.145), kind=kCustom, calls=%fused_computation.28.clone | custom fusion | bytes 90112 | tf_op jit(solution)/shard_map/jit(_take)/gather | solution.py:51
  210.6 8.8 %gather_fusion.17 = f32[2048,5]{1,0:T(8,128)} fusion(f32[5,2304]{0,1:T(8,128)} %copy.636, s32[2048]{0:T(1024)S(1)} %copy-done.147), kind=kCustom, calls=%fused_computation.29.clone | custom fusion | bytes 90112 | tf_op jit(solution)/shard_map/jit(_take)/gather | solution.py:51
  219.4 8.8 %gather_fusion.18 = f32[2048,5]{1,0:T(8,128)} fusion(f32[5,2304]{0,1:T(8,128)} %copy.636, s32[2048]{0:T(1024)S(1)} %copy-done.149), kind=kCustom, calls=%fused_computation.30.clone | custom fusion | bytes 90112 | tf_op jit(solution)/shard_map/jit(_take)/gather | solution.py:51
  228.3 8.8 %gather_fusion.19 = f32[2048,5]{1,0:T(8,128)} fusion(f32[5,2304]{0,1:T(8,128)} %copy.636, s32[2048]{0:T(1024)S(1)} %copy-done.152), kind=kCustom, calls=%fused_computation.31.clone | custom fusion | bytes 90112 | tf_op jit(solution)/shard_map/jit(_take)/gather | solution.py:51
  237.1 8.8 %gather_fusion.20 = f32[2048,5]{1,0:T(8,128)} fusion(f32[5,2304]{0,1:T(8,128)} %copy.636, s32[2048]{0:T(1024)S(1)} %copy-done.155), kind=kCustom, calls=%fused_computation.32.clone | custom fusion | bytes 90112 | tf_op jit(solution)/shard_map/jit(_take)/gather | solution.py:51
  245.9 9.2 %gather_fusion.21 = f32[2048,5]{1,0:T(8,128)} fusion(f32[5,2304]{0,1:T(8,128)} %copy.636, s32[2048]{0:T(1024)S(1)} %copy-done.158), kind=kCustom, calls=%fused_computation.33.clone | custom fusion | bytes 90112 | tf_op jit(solution)/shard_map/jit(_take)/gather | solution.py:51
  311.5 8.8 %gather_fusion.26 = f32[2048,5]{1,0:T(8,128)} fusion(f32[5,2304]{0,1:T(8,128)} %copy.655, s32[2048]{0:T(1024)S(1)} %copy-done.145), kind=kCustom, calls=%fused_computation.34.clone | custom fusion | bytes 90112 | tf_op jit(solution)/shard_map/jit(_take)/gather | solution.py:51
  320.3 8.8 %gather_fusion.27 = f32[2048,5]{1,0:T(8,128)} fusion(f32[5,2304]{0,1:T(8,128)} %copy.655, s32[2048]{0:T(1024)S(1)} %copy-done.147), kind=kCustom, calls=%fused_computation.35.clone | custom fusion | bytes 90112 | tf_op jit(solution)/shard_map/jit(_take)/gather | solution.py:51
  329.1 8.8 %gather_fusion.28 = f32[2048,5]{1,0:T(8,128)} fusion(f32[5,2304]{0,1:T(8,128)} %copy.655, s32[2048]{0:T(1024)S(1)} %copy-done.149), kind=kCustom, calls=%fused_computation.36.clone | custom fusion | bytes 90112 | tf_op jit(solution)/shard_map/jit(_take)/gather | solution.py:51
  338.0 8.8 %gather_fusion.29 = f32[2048,5]{1,0:T(8,128)} fusion(f32[5,2304]{0,1:T(8,128)} %copy.655, s32[2048]{0:T(1024)S(1)} %copy-done.152), kind=kCustom, calls=%fused_computation.37.clone | custom fusion | bytes 90112 | tf_op jit(solution)/shard_map/jit(_take)/gather | solution.py:51
  346.8 8.8 %gather_fusion.30 = f32[2048,5]{1,0:T(8,128)} fusion(f32[5,2304]{0,1:T(8,128)} %copy.655, s32[2048]{0:T(1024)S(1)} %copy-done.155), kind=kCustom, calls=%fused_computation.38.clone | custom fusion | bytes 90112 | tf_op jit(solution)/shard_map/jit(_take)/gather | solution.py:51
  355.6 9.0 %gather_fusion.31 = f32[2048,5]{1,0:T(8,128)} fusion(f32[5,2304]{0,1:T(8,128)} %copy.655, s32[2048]{0:T(1024)S(1)} %copy-done.158), kind=kCustom, calls=%fused_computation.39.clone | custom fusion | bytes 90112 | tf_op jit(solution)/shard_map/jit(_take)/gather | solution.py:51
  387.4 11.9 %scatter_custom_fusion = f32[512,5]{1,0:T(8,128)S(1)} fusion(s32[2048]{0:T(1024)} %bitcast.2143, f32[2048,5]{1,0:T(8,128)} %copy.661, f32[]{:T(128)} %constant.56.clone.1), kind=kCustom, calls=%fused_computation.679 | custom fusion | flops 10240 | bytes 10752 | tf_op jit(solution)/shard_map/scatter-add | solution.py:66
  520.1 8.4 %scatter_custom_fusion.1 = f32[128,5]{1,0:T(8,128)} fusion(s32[512]{0:T(512)} %bitcast.2159, f32[512,5]{1,0:T(8,128)S(1)} %scatter_custom_fusion, f32[5,5,512]{0,2,1:T(8,128)} %bitcast.2016, f32[5,5,512]{0,2,1:T(8,128)S(1)} %bitcast.1988, f32[5,5,512]{0,2,1:T(8,128)S(1)} %bitcast.1993, f32[5,5,512]{0,2,1:T(8,128)} %bitcast.1996, ...), kind=kCustom, calls=%fused_computation.528 | custom fusion | flops 181760 | bytes 6740992 | tf_op jit(solution)/shard_map/scatter-add | solution.py:66
  687.8 7.6 gather_fusion.84
  695.4 7.6 gather_fusion.85
  777.8 7.6 gather_fusion.95
  808.1 8.0 gather_fusion.99
  (1312 shorter events, 619.8 us)
Async XLA Ops:
  5.6 73.0 %collective-permute-start = (f32[5,64]{1,0:T(8,128)}, f32[5,64]{1,0:T(8,128)}, u32[]{:S(2)}, u32[]{:S(2)}) collective-permute-start(f32[5,64]{1,0:T(8,128)} %bitcast_multiply_fusion.59), channel_id=1, source_target_pairs={{0,2},{1,3},{2,4},{3,5},{4,6},{5,7},{6,8},{7,9},{8,10},{9,11},{10,... | collective-permute-start | bytes 3848 | tf_op jit(solution)/shard_map/ppermute | solution.py:20
  10.2 68.4 %collective-permute-start.1 = (f32[5,64]{1,0:T(8,128)}, f32[5,64]{1,0:T(8,128)}, u32[]{:S(2)}, u32[]{:S(2)}) collective-permute-start(f32[5,64]{1,0:T(8,128)} %bitcast_multiply_fusion.58), channel_id=1, source_target_pairs={{0,1},{1,2},{2,3},{3,4},{4,5},{5,6},{6,7},{7,8},{8,9},{9,10},{10,1... | collective-permute-start | bytes 3848 | tf_op jit(solution)/shard_map/ppermute | solution.py:20
  14.9 63.7 %collective-permute-start.2 = (f32[5,64]{1,0:T(8,128)}, f32[5,64]{1,0:T(8,128)}, u32[]{:S(2)}, u32[]{:S(2)}) collective-permute-start(f32[5,64]{1,0:T(8,128)} %bitcast_multiply_fusion.57), channel_id=1, source_target_pairs={{0,31},{1,0},{2,1},{3,2},{4,3},{5,4},{6,5},{7,6},{8,7},{9,8},{10,9... | collective-permute-start | bytes 3848 | tf_op jit(solution)/shard_map/ppermute | solution.py:20
  17.4 61.2 %collective-permute-start.3 = (f32[5,64]{1,0:T(8,128)}, f32[5,64]{1,0:T(8,128)}, u32[]{:S(2)}, u32[]{:S(2)}) collective-permute-start(f32[5,64]{1,0:T(8,128)} %bitcast_multiply_fusion.56), channel_id=1, source_target_pairs={{0,30},{1,31},{2,0},{3,1},{4,2},{5,3},{6,4},{7,5},{8,6},{9,7},{10,... | collective-permute-start | bytes 3848 | tf_op jit(solution)/shard_map/ppermute | solution.py:20
  22.1 279.2 %collective-permute-start.21 = (f32[5,128]{0,1:T(8,128)}, f32[5,128]{0,1:T(8,128)}, u32[]{:S(2)}, u32[]{:S(2)}) collective-permute-start(f32[5,128]{0,1:T(8,128)} %broadcast.541), channel_id=1, source_target_pairs={{0,32},{32,0},{64,96},{96,64},{128,160},{160,128},{192,224},{224,1... | collective-permute-start | bytes 7688 | tf_op jit(solution)/shard_map/ppermute | solution.py:38
  181.3 12.4 %collective-permute-start.5 = (f32[5,64]{1,0:T(8,128)}, f32[5,64]{1,0:T(8,128)S(1)}, u32[]{:S(2)}, u32[]{:S(2)}) collective-permute-start(f32[5,64]{1,0:T(8,128)} %bitcast_multiply_fusion.54), channel_id=1, source_target_pairs={{0,1},{1,2},{2,3},{3,4},{4,5},{5,6},{6,7},{7,8},{8,9},{9,10},{10,1... | collective-permute-start | bytes 3848 | tf_op jit(solution)/shard_map/ppermute | solution.py:20
  185.7 8.0 collective-permute-start.6
  289.7 14.0 %collective-permute-start.10 = (f32[5,64]{1,0:T(8,128)}, f32[5,64]{1,0:T(8,128)}, u32[]{:S(2)}, u32[]{:S(2)}) collective-permute-start(f32[5,64]{1,0:T(8,128)} %bitcast_multiply_fusion.49), channel_id=1, source_target_pairs={{0,31},{1,0},{2,1},{3,2},{4,3},{5,4},{6,5},{7,6},{8,7},{9,8},{10,9... | collective-permute-start | bytes 3848 | tf_op jit(solution)/shard_map/ppermute | solution.py:20
  293.9 10.0 %collective-permute-start.11 = (f32[5,64]{1,0:T(8,128)}, f32[5,64]{1,0:T(8,128)}, u32[]{:S(2)}, u32[]{:S(2)}) collective-permute-start(f32[5,64]{1,0:T(8,128)} %bitcast_multiply_fusion.48), channel_id=1, source_target_pairs={{0,30},{1,31},{2,0},{3,1},{4,2},{5,3},{6,4},{7,5},{8,6},{9,7},{10,... | collective-permute-start | bytes 3848 | tf_op jit(solution)/shard_map/ppermute | solution.py:20
  296.6 9.6 %collective-permute-start.9 = (f32[5,64]{1,0:T(8,128)}, f32[5,64]{1,0:T(8,128)}, u32[]{:S(2)}, u32[]{:S(2)}) collective-permute-start(f32[5,64]{1,0:T(8,128)} %bitcast_multiply_fusion.50), channel_id=1, source_target_pairs={{0,1},{1,2},{2,3},{3,4},{4,5},{5,6},{6,7},{7,8},{8,9},{9,10},{10,1... | collective-permute-start | bytes 3848 | tf_op jit(solution)/shard_map/ppermute | solution.py:20
  300.4 7.3 collective-permute-start.8
  301.9 115.0 %collective-permute-start.12 = (f32[5,32]{0,1:T(8,128)}, f32[5,32]{0,1:T(8,128)}, u32[]{:S(2)}, u32[]{:S(2)}) collective-permute-start(f32[5,32]{0,1:T(8,128)} %broadcast.539), channel_id=1, source_target_pairs={{0,1},{1,2},{2,3},{3,4},{4,5},{5,6},{6,7},{7,8},{8,9},{9,10},{10,1... | collective-permute-start | bytes 1928 | tf_op jit(solution)/shard_map/ppermute | solution.py:29
  303.7 113.2 %collective-permute-start.13 = (f32[5,32]{0,1:T(8,128)}, f32[5,32]{0,1:T(8,128)}, u32[]{:S(2)}, u32[]{:S(2)}) collective-permute-start(f32[5,32]{0,1:T(8,128)} %broadcast.539), channel_id=1, source_target_pairs={{1,0},{2,1},{3,2},{4,3},{5,4},{6,5},{7,6},{8,7},{9,8},{10,9},{11,1... | collective-permute-start | bytes 1928 | tf_op jit(solution)/shard_map/ppermute | solution.py:32
  304.7 112.2 %collective-permute-start.14 = (f32[5,512]{0,1:T(8,128)}, f32[5,512]{0,1:T(8,128)}, u32[]{:S(2)}, u32[]{:S(2)}) collective-permute-start(f32[5,512]{0,1:T(8,128)} %broadcast.538), channel_id=1, source_target_pairs={{0,32},{32,0},{64,96},{96,64},{128,160},{160,128},{192,224},{224,1... | collective-permute-start | bytes 30728 | tf_op jit(solution)/shard_map/ppermute | solution.py:38
  306.2 93.1 %collective-permute-start.22 = (f32[5,256]{0,1:T(8,128)}, f32[5,256]{0,1:T(8,128)}, u32[]{:S(2)}, u32[]{:S(2)}) collective-permute-start(f32[5,256]{0,1:T(8,128)} %concatenate.57), channel_id=1, source_target_pairs={{0,64},{32,96},{64,0},{96,32},{128,192},{160,224},{192,128},{224,1... | collective-permute-start | bytes 15368 | tf_op jit(solution)/shard_map/ppermute | solution.py:38
  446.9 8.6 %collective-permute-start.17 = (f32[5,512]{0,1:T(8,128)S(1)}, f32[5,512]{0,1:T(8,128)S(1)}, u32[]{:S(2)}, u32[]{:S(2)}) collective-permute-start(f32[5,512]{0,1:T(8,128)S(1)} %add_multiply_fusion), channel_id=1, source_target_pairs={{0,32},{32,0},{64,96},{96,64},{128,160},{160,128},{192,224},{224,1... | collective-permute-start | bytes 30728 | tf_op jit(solution)/shard_map/ppermute | solution.py:38
  581.6 13.2 %collective-permute-start.29 = (f32[5,512]{0,1:T(8,128)S(1)}, f32[5,512]{0,1:T(8,128)S(1)}, u32[]{:S(2)}, u32[]{:S(2)}) collective-permute-start(f32[5,512]{0,1:T(8,128)S(1)} %bitcast_add_fusion), channel_id=1, source_target_pairs={{0,32},{32,0},{64,96},{96,64},{128,160},{160,128},{192,224},{224,1... | collective-permute-start | bytes 30728 | tf_op jit(solution)/shard_map/ppermute | solution.py:38
  583.1 11.7 %collective-permute-start.27 = (f32[5,32]{0,1:T(8,128)S(1)}, f32[5,32]{0,1:T(8,128)S(1)}, u32[]{:S(2)}, u32[]{:S(2)}) collective-permute-start(f32[5,32]{0,1:T(8,128)S(1)} %get-tuple-element.497), channel_id=1, source_target_pairs={{0,1},{1,2},{2,3},{3,4},{4,5},{5,6},{6,7},{7,8},{8,9},{9,10},{10,1... | collective-permute-start | bytes 1928 | tf_op jit(solution)/shard_map/ppermute | solution.py:29
  587.7 7.1 collective-permute-start.28
  624.4 7.1 collective-permute-start.32
  670.6 11.6 %collective-permute-start.34 = (f32[5,64]{1,0:T(8,128)S(1)}, f32[5,64]{1,0:T(8,128)S(1)}, u32[]{:S(2)}, u32[]{:S(2)}) collective-permute-start(f32[5,64]{1,0:T(8,128)S(1)} %bitcast_multiply_fusion.46), channel_id=1, source_target_pairs={{0,1},{1,2},{2,3},{3,4},{4,5},{5,6},{6,7},{7,8},{8,9},{9,10},{10,1... | collective-permute-start | bytes 3848 | tf_op jit(solution)/shard_map/ppermute | solution.py:20
  670.8 11.4 %collective-permute-start.35 = (f32[5,64]{1,0:T(8,128)S(1)}, f32[5,64]{1,0:T(8,128)S(1)}, u32[]{:S(2)}, u32[]{:S(2)}) collective-permute-start(f32[5,64]{1,0:T(8,128)S(1)} %bitcast_multiply_fusion.45), channel_id=1, source_target_pairs={{0,31},{1,0},{2,1},{3,2},{4,3},{5,4},{6,5},{7,6},{8,7},{9,8},{10,9... | collective-permute-start | bytes 3848 | tf_op jit(solution)/shard_map/ppermute | solution.py:20
  755.7 9.0 %collective-permute-start.38 = (f32[5,64]{1,0:T(8,128)S(1)}, f32[5,64]{1,0:T(8,128)S(1)}, u32[]{:S(2)}, u32[]{:S(2)}) collective-permute-start(f32[5,64]{1,0:T(8,128)S(1)} %bitcast_multiply_fusion.42), channel_id=1, source_target_pairs={{0,1},{1,2},{2,3},{3,4},{4,5},{5,6},{6,7},{7,8},{8,9},{9,10},{10,1... | collective-permute-start | bytes 3848 | tf_op jit(solution)/shard_map/ppermute | solution.py:20
  756.4 8.2 collective-permute-start.39
  (413 other events, 4306.0 us)
where the time goes:
time: 852 us; the launch traced here: 838 us
  local copies, waits for them, and re-layouts  605 us (71%)
  other arithmetic  133 us (16%)
  starting transfers between devices  74.5 us (9%)
  waiting for transfers between devices  19.7 us (2%)
    gather x78, local copies, waits for them, and re-layouts, apply_rows(): picked = jnp.take(extended, columns[neighbor], axis=1)  364 us
    slice x96, local copies, waits for them, and re-layouts, block_product(): total = blocks[:, 0] * vectors[0]  126 us
    select_n x81, other arithmetic, apply_rows(): picked = jnp.take(extended, columns[neighbor], axis=1)  41.8 us
    unnamed x814, local copies, waits for them, and re-layouts  38.3 us
    gather x40, local copies, waits for them, and re-layouts, fine_extend(): jnp.take(field, send[peer_slot], axis=1)  37 us
    ppermute x20, starting transfers between devices, passed_along(): return lax.ppermute(x, axis, [(i, (i + by) % size) for i in range(size)])  34.3 us
    scatter-add x2, other arithmetic, restrict_rows(): return jax.ops.segment_sum(residual.T, aggregate, num_segments=number).T  20.3 us
    ppermute x5, starting transfers between devices, with_halo(): lax.ppermute(lax.slice_in_dim(block, 0, width, axis=dim), axis, backward)  18.5 us
  transfers between devices with their start and end apart: 41, of which 7 were waited for; matrix products, arithmetic and copies ran while one was open for 47% of the time, Pallas kernels for 0%

commit v1 on v0

v1 whole, which is shorter than its diff:
```python
import functools

import jax
import jax.numpy as jnp
from jax import lax
from jax.experimental import pallas as pl
from jax.experimental.pallas import tpu as pltpu
from jax.sharding import PartitionSpec as P

ROWS_FINE = 2048
ROWS_MID = 512
ROWS_COARSE = 128
SLOT_ROWS = 64
RIM_ROWS = 32
LANES = 128
OFFSETS = (-2, -1, 1, 2)
RELAX = 0.8
F32 = jnp.float32


def lane_pick(chunk, index):
    return jnp.take_along_axis(chunk, index, axis=1, mode="promise_in_bounds")


def pick(table, index_row, chunks):
    index = jnp.broadcast_to(index_row, (8, LANES))
    low = index & (LANES - 1)
    high = index >> 7
    level = [lane_pick(table(t), low) for t in range(chunks)]
    bit = 0
    while len(level) > 1:
        odd = ((high >> bit) & 1) == 1
        level = [
            jnp.where(odd, level[i + 1], level[i]) if i + 1 < len(level) else level[i]
            for i in range(0, len(level), 2)
        ]
        bit += 1
    return level[0]


def padded(value):
    return jnp.concatenate([value, jnp.zeros((3, value.shape[1]), value.dtype)], axis=0)


def rows_of(parts):
    return jnp.concatenate([jnp.sum(part, axis=0, keepdims=True) for part in parts], axis=0)


def apply_chunk(diag, coupling, columns, table, chunks, rows, remap=None):
    own = table(None)
    parts = [diag[i, :, rows] * own for i in range(5)]
    for n in range(6):
        index = columns[n : n + 1, rows]
        if remap is not None:
            index = remap(index)
        picked = pick(table, index, chunks)[:5]
        for i in range(5):
            parts[i] = parts[i] + coupling[n, i, :, rows] * picked
    return rows_of(parts)


def inverse_chunk(inverse, value, rows):
    return rows_of([inverse[i, :, rows] * value for i in range(5)])


def lane_slice(c):
    return pl.ds(pl.multiple_of(c * LANES, LANES), LANES)


def split3(value):
    first = value.astype(jnp.bfloat16)
    rest = value - first.astype(F32)
    second = rest.astype(jnp.bfloat16)
    third = (rest - second.astype(F32)).astype(jnp.bfloat16)
    return first, second, third


def restrict(residual, aggregate, number, store):
    rows = aggregate.shape[1]
    groups = number // LANES
    total = jnp.zeros((3 * 8 * groups, LANES), F32)
    step = min(rows, 512)
    for start in range(0, rows, step):
        index = aggregate[:, start : start + step]
        value = residual(start, step)
        high = index >> 7
        low = index & (LANES - 1)
        left = []
        for piece in split3(value):
            wide = piece.astype(F32)
            left += [jnp.where(high == h, wide, 0.0) for h in range(groups)]
        left = jnp.concatenate(left, axis=0).astype(jnp.bfloat16)
        lanes = lax.broadcasted_iota(jnp.int32, (LANES, step), 0)
        hot = jnp.where(lanes == low, 1.0, 0.0).astype(jnp.bfloat16)
        total = total + lax.dot_general(
            left, hot, (((1,), (1,)), ((), ())), preferred_element_type=F32
        )
    size = 8 * groups
    summed = total[:size] + total[size : 2 * size] + total[2 * size :]
    for h in range(groups):
        store(h, summed[h * 8 : h * 8 + 8])


def load_fine(x, received, ext):
    for c in range(ROWS_FINE // LANES):
        ext[c, 0:5] = x[:, c * LANES : (c + 1) * LANES]
    for j in range(4):
        lane = (j % 2) * SLOT_ROWS
        ext[16 + j // 2, 0:5, lane : lane + SLOT_ROWS] = received[j][...]


def pack_sends(table, send, count, outs):
    position = lax.broadcasted_iota(jnp.int32, (1, SLOT_ROWS), 1)
    for pair in range(2):
        index = jnp.concatenate([send[2 * pair : 2 * pair + 1], send[2 * pair + 1 : 2 * pair + 2]], axis=1)
        picked = pick(table, index, 16)[:5]
        for half in range(2):
            j = 2 * pair + half
            live = (position < count[j]).astype(F32)
            outs[j][...] = picked[:, half * SLOT_ROWS : (half + 1) * SLOT_ROWS] * live


def send_kernel(x, send, count, s0, s1, s2, s3):
    pack_sends(
        lambda t: padded(x[:, t * LANES : (t + 1) * LANES]), send, count, (s0, s1, s2, s3)
    )


def fine_sweep_body(x, b, diag, inverse, coupling, columns, ext, result):
    def body(c, carry):
        rows = lane_slice(c)
        own = ext[c][:5]
        table = lambda t: own if t is None else ext[t]
        image = apply_chunk(diag, coupling, columns, table, 18, rows)
        change = inverse_chunk(inverse, b[:, rows] - image, rows)
        result(c, own + RELAX * change)
        return carry

    lax.fori_loop(0, 16, body, 0)


def fine_kernel(last, x, b, diag, inverse, coupling, columns, send, count, r0, r1, r2, r3, *rest):
    if last:
        new, ext = rest
        outs = None
    else:
        new, s0, s1, s2, s3, ext, fresh = rest
        outs = (s0, s1, s2, s3)
    load_fine(x, (r0, r1, r2, r3), ext)

    def result(c, value):
        new[:, lane_slice(c)] = value
        if not last:
            fresh[c, 0:5] = value

    fine_sweep_body(x, b, diag, inverse, coupling, columns, ext, result)
    if not last:
        pack_sends(lambda t: fresh[t], send, count, outs)


def down_kernel(
    x, b, diag, coupling, columns, aggregate, m_inverse, r0, r1, r2, r3, rhs, e, low_rim, high_rim, ext, residual
):
    load_fine(x, (r0, r1, r2, r3), ext)
    residual[5:8, :] = jnp.zeros((3, ROWS_FINE), F32)

    def body(c, carry):
        rows = lane_slice(c)
        own = ext[c][:5]
        table = lambda t: own if t is None else ext[t]
        image = apply_chunk(diag, coupling, columns, table, 18, rows)
        residual[0:5, rows] = b[:, rows] - image
        return carry

    lax.fori_loop(0, 16, body, 0)

    def store(h, value):
        rows = slice(h * LANES, (h + 1) * LANES)
        rhs[:, rows] = value[:5]
        e[:, rows] = RELAX * inverse_chunk(m_inverse, value[:5], rows)

    restrict(lambda s, n: residual[:, s : s + n], aggregate, ROWS_MID, store)
    send_rims(e, low_rim, high_rim)


def send_rims(e, first, last):
    first[...] = e[:, 0:RIM_ROWS]
    last[...] = e[:, ROWS_MID - RIM_ROWS : ROWS_MID]


def middle_remap(index):
    own = index - RIM_ROWS
    left = index + 2 * ROWS_MID
    right = index + ROWS_MID
    partner = index - 2 * RIM_ROWS
    return jnp.where(
        index < RIM_ROWS,
        left,
        jnp.where(
            index < RIM_ROWS + ROWS_MID,
            own,
            jnp.where(index < 2 * RIM_ROWS + ROWS_MID, right, partner),
        ),
    )


def load_middle(e, left, right, partner, ext):
    for c in range(4):
        ext[c, 0:5] = e[:, c * LANES : (c + 1) * LANES]
        ext[4 + c, 0:5] = partner[:, c * LANES : (c + 1) * LANES]
    ext[8, 0:5, 0:RIM_ROWS] = left[...]
    ext[8, 0:5, RIM_ROWS : 2 * RIM_ROWS] = right[...]


def middle_rows(e_table, c, diag, coupling, columns):
    rows = slice(c * LANES, (c + 1) * LANES)
    own = e_table[c][:5]
    table = lambda t: own if t is None else e_table[t]
    return rows, own, apply_chunk(diag, coupling, columns, table, 9, rows, middle_remap)


def middle_kernel(e, rhs, diag, inverse, coupling, columns, left, right, partner, new, first, last, ext):
    load_middle(e, left, right, partner, ext)
    for c in range(4):
        rows, own, image = middle_rows(ext, c, diag, coupling, columns)
        new[:, rows] = own + RELAX * inverse_chunk(inverse, rhs[:, rows] - image, rows)
    send_rims(new, first, last)


def coarse_down_kernel(
    e, rhs, diag, coupling, columns, left, right, partner, aggregate, c_inverse, c_rhs, c_new, ext, residual
):
    load_middle(e, left, right, partner, ext)
    residual[5:8, :] = jnp.zeros((3, ROWS_MID), F32)
    for c in range(4):
        rows, own, image = middle_rows(ext, c, diag, coupling, columns)
        residual[0:5, rows] = rhs[:, rows] - image

    def store(h, value):
        rows = slice(0, LANES)
        c_rhs[...] = value[:5]
        c_new[...] = RELAX * inverse_chunk(c_inverse, value[:5], rows)

    restrict(lambda s, n: residual[:, s : s + n], aggregate, ROWS_COARSE, store)


def coarse_rows(c_field, others, diag, inverse, coupling, columns, rhs):
    rows = slice(0, LANES)
    members = [padded(r[...]) for r in (c_field,) + others]
    own = c_field[...]
    table = lambda t: own if t is None else members[t]
    image = apply_chunk(diag, coupling, columns, table, 4, rows)
    return own + RELAX * inverse_chunk(inverse, rhs[...] - image, rows)


def coarse_kernel(field, rhs, diag, inverse, coupling, columns, p1, p2, p3, new):
    new[...] = coarse_rows(field, (p1, p2, p3), diag, inverse, coupling, columns, rhs)


def coarse_up_kernel(field, rhs, diag, inverse, coupling, columns, p1, p2, p3, e, aggregate, new, first, last):
    done = padded(coarse_rows(field, (p1, p2, p3), diag, inverse, coupling, columns, rhs))
    for c in range(4):
        rows = slice(c * LANES, (c + 1) * LANES)
        new[:, rows] = e[:, rows] + pick(lambda t: done, aggregate[:, rows], 1)[:5]
    send_rims(new, first, last)


def middle_up_kernel(
    e, rhs, diag, inverse, coupling, columns, left, right, partner, x, aggregate, send, count,
    new, s0, s1, s2, s3, ext, done, fresh
):
    load_middle(e, left, right, partner, ext)
    for c in range(4):
        rows, own, image = middle_rows(ext, c, diag, coupling, columns)
        done[c, 0:5] = own + RELAX * inverse_chunk(inverse, rhs[:, rows] - image, rows)
    for c in range(16):
        rows = slice(c * LANES, (c + 1) * LANES)
        value = x[:, rows] + pick(lambda t: done[t], aggregate[:, rows], 4)[:5]
        new[:, rows] = value
        fresh[c, 0:5] = value
    pack_sends(lambda t: fresh[t], send, count, (s0, s1, s2, s3))


VMEM = pl.BlockSpec(memory_space=pltpu.VMEM)
SMEM = pl.BlockSpec(memory_space=pltpu.SMEM)


def call(name, kernel, args, shapes, scratch=(), scalars=()):
    return pl.pallas_call(
        kernel,
        name=name,
        out_shape=[jax.ShapeDtypeStruct(s, F32) for s in shapes],
        in_specs=[SMEM if i in scalars else VMEM for i in range(len(args))],
        out_specs=[VMEM] * len(shapes),
        scratch_shapes=[pltpu.VMEM(s, F32) for s in scratch],
        compiler_params=pltpu.CompilerParams(vmem_limit_bytes=16 * 1024 * 1024),
    )(*args)


def passed_along(x, by):
    size = lax.axis_size("dom")
    return lax.ppermute(x, "dom", [(i, (i + by) % size) for i in range(size)])


def group_swap(x, mask):
    return lax.ppermute(x, "grp", [(i, i ^ mask) for i in range(lax.axis_size("grp"))])


def per_device(
    right_side, initial_guess, fine_diag, fine_inverse, fine_coupling, fine_columns, fine_send, fine_count,
    fine_aggregate, middle_diag, middle_inverse, middle_coupling, middle_columns, middle_aggregate,
    coarse_diag, coarse_inverse, coarse_coupling, coarse_columns,
):
    b, x = right_side[0, 0], initial_guess[0, 0]
    f_mats = (fine_diag[0, 0], fine_inverse[0, 0], fine_coupling[0, 0], fine_columns[0, 0])
    f_send, f_count, f_aggregate = fine_send[0, 0], fine_count[0, 0], fine_aggregate[0]
    m_mats = (middle_diag[0, 0], middle_inverse[0, 0], middle_coupling[0, 0], middle_columns[0, 0])
    m_aggregate = middle_aggregate[0]
    c_mats = (coarse_diag[0, 0], coarse_inverse[0, 0], coarse_coupling[0, 0], coarse_columns[0, 0])

    slot = (5, SLOT_ROWS)
    fine = (5, ROWS_FINE)
    mid = (5, ROWS_MID)
    coarse = (5, ROWS_COARSE)
    rim = (5, RIM_ROWS)
    f_ext, f_fresh = (18, 8, LANES), (16, 8, LANES)
    m_ext = (9, 8, LANES)

    def fine_exchange(sends):
        return [passed_along(sends[3 - j], -offset) for j, offset in enumerate(OFFSETS)]

    def middle_exchange(e, first, last):
        return [passed_along(last, 1), passed_along(first, -1), group_swap(e, 1)]

    def coarse_exchange(c):
        return [group_swap(c, mask) for mask in (1, 2, 3)]

    def fine_sweep(name, x, sends, last=False):
        received = fine_exchange(sends)
        out = call(
            name,
            functools.partial(fine_kernel, last),
            (x, b) + f_mats + (f_send, f_count, *received),
            [fine] if last else [fine] + [slot] * 4,
            [f_ext] if last else [f_ext, f_fresh],
            scalars=(7,),
        )
        return out[0], out[1:]

    sends = call("send", send_kernel, (x, f_send, f_count), [slot] * 4, scalars=(2,))
    x, sends = fine_sweep("fine_1", x, sends)
    x, sends = fine_sweep("fine_2", x, sends)
    rhs, e, first, last = call(
        "down",
        down_kernel,
        (x, b, f_mats[0], f_mats[2], f_mats[3], f_aggregate, m_mats[1], *fine_exchange(sends)),
        [mid, mid, rim, rim],
        [f_ext, (8, ROWS_FINE)],
    )

    def middle_sweep(name, e, first, last):
        return call(
            name, middle_kernel, (e, rhs) + m_mats + tuple(middle_exchange(e, first, last)),
            [mid, rim, rim], [m_ext],
        )

    e, first, last = middle_sweep("middle_2", e, first, last)
    c_rhs, c = call(
        "coarse_down",
        coarse_down_kernel,
        (e, rhs, m_mats[0], m_mats[2], m_mats[3], *middle_exchange(e, first, last), m_aggregate, c_mats[1]),
        [coarse, coarse],
        [m_ext, (8, ROWS_MID)],
    )
    (c,) = call("coarse_2", coarse_kernel, (c, c_rhs) + c_mats + tuple(coarse_exchange(c)), [coarse])
    e, first, last = call(
        "coarse_3",
        coarse_up_kernel,
        (c, c_rhs) + c_mats + tuple(coarse_exchange(c)) + (e, m_aggregate),
        [mid, rim, rim],
    )
    e, first, last = middle_sweep("middle_3", e, first, last)
    out = call(
        "middle_4",
        middle_up_kernel,
        (e, rhs) + m_mats + tuple(middle_exchange(e, first, last)) + (x, f_aggregate, f_send, f_count),
        [fine] + [slot] * 4,
        [m_ext, (4, 8, LANES), f_fresh],
        scalars=(12,),
    )
    x, sends = out[0], out[1:]
    x, sends = fine_sweep("fine_4", x, sends)
    x, _ = fine_sweep("fine_5", x, sends, last=True)
    return x[None, None]


def solution(mesh):
    def spec(rank):
        return P("grp", "dom", *([None] * (rank - 2)))

    ranks = (4, 4, 5, 5, 6, 4, 4, 3, 3, 5, 5, 6, 4, 3, 5, 5, 6, 4)
    return jax.shard_map(
        per_device,
        mesh=mesh,
        in_specs=tuple(spec(rank) for rank in ranks),
        out_specs=spec(4),
        check_vma=False,
    )
```

time: 852 us -> 126 us (0.15); the launches traced: 838 us -> 124 us
  local copies, waits for them, and re-layouts: 605 us -> 6.04 us
  other arithmetic: 133 us -> 0 us
  Pallas kernels: 0 us -> 26.1 us
    gather x121 -> x0, local copies, waits for them, and re-layouts: 408 us -> none  [the longest x78 364 us: apply_rows(): picked = jnp.take(extended, columns[neighbor], axis=1)]
    slice x108 -> x0, local copies, waits for them, and re-layouts: 131 us -> none  [the longest x96 126 us: block_product(): total = blocks[:, 0] * vectors[0]]
    select_n x84 -> x0, other arithmetic: 43 us -> none  [the longest x81 41.8 us: apply_rows(): picked = jnp.take(extended, columns[neighbor], axis=1)]
    unnamed x814 -> x42, local copies, waits for them, and re-layouts: 38.3 us -> 3.46 us
    pallas_call x0 -> x12, Pallas kernels: none -> 26.1 us  [call(): pl.pallas_call(kernel, name=name, out_shape=[jax.ShapeDtypeStruct(s, F32)...]
    scatter-add x2 -> x0, other arithmetic: 20.3 us -> none  [restrict_rows(): return jax.ops.segment_sum(residual.T, aggregate, num_segments=number).T]
    sub x11 -> x0, other arithmetic: 18.3 us -> none  [sweep_rows(): return field + relaxation * block_product(inverse, target - image)]
    concatenate x13 -> x0, local copies, waits for them, and re-layouts: 15.2 us -> none  [the longest x10 12.7 us: fine_extend(): return jnp.concatenate([field] + blocks, axis=-1)]
  transfers between devices with their start and end apart: 41 -> 38, of which waited for: 7 -> 17; matrix products, arithmetic and copies ran while one was open for 47% -> 3% of each run, Pallas kernels for 0% -> 0%
where the time goes in v1:
time: 126 us; the launch traced here: 124 us
  starting transfers between devices  74.7 us (59%)
  Pallas kernels  26.1 us (21%)
  waiting for transfers between devices  16.9 us (13%)
  local copies, waits for them, and re-layouts  6.04 us (5%)
    ppermute x28, starting transfers between devices, passed_along(): return lax.ppermute(x, 'dom', [(i, (i + by) % size) for i in range(size)])  64.6 us
    pallas_call x12, Pallas kernels, call(): pl.pallas_call(kernel, name=name, out_shape=[jax.ShapeDtypeStruct(s, F32)...  26.1 us
    ppermute x28, waiting for transfers between devices, passed_along(): return lax.ppermute(x, 'dom', [(i, (i + by) % size) for i in range(size)])  11.7 us
    ppermute x10, starting transfers between devices, group_swap(): lax.ppermute(x, 'grp', [(i, i ^ mask) for i in range(lax.axis_size('grp'))])  10.1 us
    ppermute x10, waiting for transfers between devices, group_swap(): lax.ppermute(x, 'grp', [(i, i ^ mask) for i in range(lax.axis_size('grp'))])  5.19 us
    unnamed x42, local copies, waits for them, and re-layouts  3.46 us
  transfers between devices with their start and end apart: 38, of which 17 were waited for; matrix products, arithmetic and copies ran while one was open for 3% of the time, Pallas kernels for 0%

profile of v1, /device:TPU:1, one launch (start us, length us, event | category | flops | bytes accessed | tf_op | source)
XLA Modules:
  0.0 124.1 jit_solution(1533571322900764574)
XLA Ops:
  2.9 2.1 %collective-permute-start = (f32[5,64]{1,0:T(8,128)S(1)}, f32[5,64]{1,0:T(8,128)S(1)}, u32[]{:S(2)}, u32[]{:S(2)}) collective-permute-start(f32[5,64]{1,0:T(8,128)S(1)} %get-tuple-element.44), channel_id=1, source_target_pairs={{0,2},{1,3},{2,4},{3,5},{4,6},{5,7},{6,8},{7,9},{8,10},{9,11},{10,... | collective-permute-start | bytes 3848 | tf_op jit(solution)/shard_map/ppermute | solution.py:302
  5.1 2.1 %collective-permute-start.1 = (f32[5,64]{1,0:T(8,128)S(1)}, f32[5,64]{1,0:T(8,128)S(1)}, u32[]{:S(2)}, u32[]{:S(2)}) collective-permute-start(f32[5,64]{1,0:T(8,128)S(1)} %get-tuple-element.45), channel_id=1, source_target_pairs={{0,1},{1,2},{2,3},{3,4},{4,5},{5,6},{6,7},{7,8},{8,9},{9,10},{10,1... | collective-permute-start | bytes 3848 | tf_op jit(solution)/shard_map/ppermute | solution.py:302
  7.2 4.0 %collective-permute-start.3 = (f32[5,64]{1,0:T(8,128)S(1)}, f32[5,64]{1,0:T(8,128)S(1)}, u32[]{:S(2)}, u32[]{:S(2)}) collective-permute-start(f32[5,64]{1,0:T(8,128)S(1)} %get-tuple-element.47), channel_id=1, source_target_pairs={{0,30},{1,31},{2,0},{3,1},{4,2},{5,3},{6,4},{7,5},{8,6},{9,7},{10,... | collective-permute-start | bytes 3848 | tf_op jit(solution)/shard_map/ppermute | solution.py:302
  12.5 1.9 %copy.63 = f32[1,1,6,5,5,2048]{5,4,3,2,0,1:T(8,128)S(1)} copy(f32[1,1,6,5,5,2048]{5,1,4,3,2,0:T(1,128)} %param.22) | data formatting | bytes 2457600 | tf_op jit(solution)/shard_map/squeeze | solution.py:315
  14.5 4.6 %fine_1.1 = (f32[5,2048]{1,0:T(8,128)S(1)}, f32[5,64]{1,0:T(8,128)S(1)}, f32[5,64]{1,0:T(8,128)S(1)}, f32[5,64]{1,0:T(8,128)S(1)}, f32[5,64]{1,0:T(8,128)S(1)}) custom-call(f32[5,2048]{1,0:T(8,128)S(1)} %bitcast.78, f32[5,2048]{1,0:T(8,128)S(1)} %bitcast.62, f32[5,5,2048]{2,1,0:T(8,128)S(1)} %get-tuple-element.84.diag, ...), custom_call_target="tpu_custom_call" | custom-call | tf_op jit(solution)/shard_map/fine_1/pallas_call | solution.py:289
  19.1 1.8 %collective-permute-start.5 = (f32[5,64]{1,0:T(8,128)S(1)}, f32[5,64]{1,0:T(8,128)S(1)}, u32[]{:S(2)}, u32[]{:S(2)}) collective-permute-start(f32[5,64]{1,0:T(8,128)S(1)} %get-tuple-element.50), channel_id=1, source_target_pairs={{0,1},{1,2},{2,3},{3,4},{4,5},{5,6},{6,7},{7,8},{8,9},{9,10},{10,1... | collective-permute-start | bytes 3848 | tf_op jit(solution)/shard_map/ppermute | solution.py:302
  21.3 4.9 %collective-permute-start.7 = (f32[5,64]{1,0:T(8,128)S(1)}, f32[5,64]{1,0:T(8,128)S(1)}, u32[]{:S(2)}, u32[]{:S(2)}) collective-permute-start(f32[5,64]{1,0:T(8,128)S(1)} %get-tuple-element.52), channel_id=1, source_target_pairs={{0,30},{1,31},{2,0},{3,1},{4,2},{5,3},{6,4},{7,5},{8,6},{9,7},{10,... | collective-permute-start | bytes 3848 | tf_op jit(solution)/shard_map/ppermute | solution.py:302
  26.9 4.6 %fine_2.1 = (f32[5,2048]{1,0:T(8,128)S(1)}, f32[5,64]{1,0:T(8,128)S(1)}, f32[5,64]{1,0:T(8,128)S(1)}, f32[5,64]{1,0:T(8,128)S(1)}, f32[5,64]{1,0:T(8,128)S(1)}) custom-call(f32[5,2048]{1,0:T(8,128)S(1)} %get-tuple-element.48.x, f32[5,2048]{1,0:T(8,128)S(1)} %bitcast.63, f32[5,5,2048]{2,1,0:T(8,128)S(1)} %get-tuple-element.84.diag, ...), custom_call_target="tpu_custom_call" | custom-call | tf_op jit(solution)/shard_map/fine_2/pallas_call | solution.py:289
  31.5 3.0 %collective-permute-start.10 = (f32[5,64]{1,0:T(8,128)S(1)}, f32[5,64]{1,0:T(8,128)S(1)}, u32[]{:S(2)}, u32[]{:S(2)}) collective-permute-start(f32[5,64]{1,0:T(8,128)S(1)} %get-tuple-element.56), channel_id=1, source_target_pairs={{0,31},{1,0},{2,1},{3,2},{4,3},{5,4},{6,5},{7,6},{8,7},{9,8},{10,9... | collective-permute-start | bytes 3848 | tf_op jit(solution)/shard_map/ppermute | solution.py:302
  34.5 5.0 %collective-permute-start.11 = (f32[5,64]{1,0:T(8,128)S(1)}, f32[5,64]{1,0:T(8,128)S(1)}, u32[]{:S(2)}, u32[]{:S(2)}) collective-permute-start(f32[5,64]{1,0:T(8,128)S(1)} %get-tuple-element.57), channel_id=1, source_target_pairs={{0,30},{1,31},{2,0},{3,1},{4,2},{5,3},{6,4},{7,5},{8,6},{9,7},{10,... | collective-permute-start | bytes 3848 | tf_op jit(solution)/shard_map/ppermute | solution.py:302
  40.3 5.0 %collective-permute-done.8.r0 = f32[5,64]{1,0:T(8,128)S(1)} collective-permute-done((f32[5,64]{1,0:T(8,128)S(1)}, f32[5,64]{1,0:T(8,128)S(1)}, u32[]{:S(2)}, u32[]{:S(2)}) %collective-permute-start.8) | collective-permute-done | bytes 1312 | tf_op jit(solution)/shard_map/ppermute | solution.py:302
  45.3 4.0 %down.1 = (f32[5,512]{1,0:T(8,128)S(1)}, f32[5,512]{1,0:T(8,128)S(1)}, f32[5,32]{1,0:T(8,128)S(1)}, f32[5,32]{1,0:T(8,128)S(1)}) custom-call(f32[5,2048]{1,0:T(8,128)S(1)} %get-tuple-element.53.x, f32[5,2048]{1,0:T(8,128)S(1)} %bitcast.64, f32[5,5,2048]{2,1,0:T(8,128)S(1)} %get-tuple-element.84.diag, f32[6,5,5,2048]{3,2,1,0:T(8,128)S(1)} %bitcast.50, ...), custom_call_target="tpu_custom_call" | custom-call | tf_op jit(solution)/shard_map/down/pallas_call | solution.py:289
  54.7 5.1 %collective-permute-start.16 = (f32[5,32]{1,0:T(8,128)S(1)}, f32[5,32]{1,0:T(8,128)S(1)}, u32[]{:S(2)}, u32[]{:S(2)}) collective-permute-start(f32[5,32]{1,0:T(8,128)S(1)} %get-tuple-element.64), channel_id=1, source_target_pairs={{0,31},{1,0},{2,1},{3,2},{4,3},{5,4},{6,5},{7,6},{8,7},{9,8},{10,9... | collective-permute-start | bytes 1928 | tf_op jit(solution)/shard_map/ppermute | solution.py:302
  61.5 3.0 %collective-permute-start.19 = (f32[5,128]{1,0:T(8,128)S(1)}, f32[5,128]{1,0:T(8,128)S(1)}, u32[]{:S(2)}, u32[]{:S(2)}) collective-permute-start(f32[5,128]{1,0:T(8,128)S(1)} %get-tuple-element.65.field), channel_id=1, source_target_pairs={{0,64},{32,96},{64,0},{96,32},{128,192},{160,224},{192,128},{224,1... | collective-permute-start | bytes 7688 | tf_op jit(solution)/shard_map/ppermute | solution.py:306
  65.8 3.0 %collective-permute-done.20.p3 = f32[5,128]{1,0:T(8,128)S(1)} collective-permute-done((f32[5,128]{1,0:T(8,128)S(1)}, f32[5,128]{1,0:T(8,128)S(1)}, u32[]{:S(2)}, u32[]{:S(2)}) %collective-permute-start.20) | collective-permute-done | bytes 2592 | tf_op jit(solution)/shard_map/ppermute | solution.py:306
  69.6 2.9 %collective-permute-start.23 = (f32[5,128]{1,0:T(8,128)S(1)}, f32[5,128]{1,0:T(8,128)S(1)}, u32[]{:S(2)}, u32[]{:S(2)}) collective-permute-start(f32[5,128]{1,0:T(8,128)S(1)} %coarse_2.1.field), channel_id=1, source_target_pairs={{0,96},{32,64},{64,32},{96,0},{128,224},{160,192},{192,160},{224,1... | collective-permute-start | bytes 7688 | tf_op jit(solution)/shard_map/ppermute | solution.py:306
  74.8 8.5 %collective-permute-start.25 = (f32[5,32]{1,0:T(8,128)S(1)}, f32[5,32]{1,0:T(8,128)S(1)}, u32[]{:S(2)}, u32[]{:S(2)}) collective-permute-start(f32[5,32]{1,0:T(8,128)S(1)} %get-tuple-element.69), channel_id=1, source_target_pairs={{0,31},{1,0},{2,1},{3,2},{4,3},{5,4},{6,5},{7,6},{8,7},{9,8},{10,9... | collective-permute-start | bytes 1928 | tf_op jit(solution)/shard_map/ppermute | solution.py:302
  86.3 5.8 %collective-permute-start.28 = (f32[5,32]{1,0:T(8,128)S(1)}, f32[5,32]{1,0:T(8,128)S(1)}, u32[]{:S(2)}, u32[]{:S(2)}) collective-permute-start(f32[5,32]{1,0:T(8,128)S(1)} %get-tuple-element.72), channel_id=1, source_target_pairs={{0,31},{1,0},{2,1},{3,2},{4,3},{5,4},{6,5},{7,6},{8,7},{9,8},{10,9... | collective-permute-start | bytes 1928 | tf_op jit(solution)/shard_map/ppermute | solution.py:302
  94.4 5.6 %collective-permute-start.32 = (f32[5,64]{1,0:T(8,128)S(1)}, f32[5,64]{1,0:T(8,128)S(1)}, u32[]{:S(2)}, u32[]{:S(2)}) collective-permute-start(f32[5,64]{1,0:T(8,128)S(1)} %get-tuple-element.76), channel_id=1, source_target_pairs={{0,31},{1,0},{2,1},{3,2},{4,3},{5,4},{6,5},{7,6},{8,7},{9,8},{10,9... | collective-permute-start | bytes 3848 | tf_op jit(solution)/shard_map/ppermute | solution.py:302
  100.0 5.0 %collective-permute-start.33 = (f32[5,64]{1,0:T(8,128)S(1)}, f32[5,64]{1,0:T(8,128)S(1)}, u32[]{:S(2)}, u32[]{:S(2)}) collective-permute-start(f32[5,64]{1,0:T(8,128)S(1)} %get-tuple-element.77), channel_id=1, source_target_pairs={{0,30},{1,31},{2,0},{3,1},{4,2},{5,3},{6,4},{7,5},{8,6},{9,7},{10,... | collective-permute-start | bytes 3848 | tf_op jit(solution)/shard_map/ppermute | solution.py:302
  105.8 4.6 %fine_4.1 = (f32[5,2048]{1,0:T(8,128)S(1)}, f32[5,64]{1,0:T(8,128)S(1)}, f32[5,64]{1,0:T(8,128)S(1)}, f32[5,64]{1,0:T(8,128)S(1)}, f32[5,64]{1,0:T(8,128)S(1)}) custom-call(f32[5,2048]{1,0:T(8,128)S(1)} %get-tuple-element.73.x, f32[5,2048]{1,0:T(8,128)S(1)} %bitcast.65, f32[5,5,2048]{2,1,0:T(8,128)S(1)} %get-tuple-element.84.diag, ...), custom_call_target="tpu_custom_call" | custom-call | tf_op jit(solution)/shard_map/fine_4/pallas_call | solution.py:289
  110.4 2.3 %collective-permute-start.35 = (f32[5,64]{1,0:T(8,128)S(1)}, f32[5,64]{1,0:T(8,128)S(1)}, u32[]{:S(2)}, u32[]{:S(2)}) collective-permute-start(f32[5,64]{1,0:T(8,128)S(1)} %get-tuple-element.80), channel_id=1, source_target_pairs={{0,1},{1,2},{2,3},{3,4},{4,5},{5,6},{6,7},{7,8},{8,9},{9,10},{10,1... | collective-permute-start | bytes 3848 | tf_op jit(solution)/shard_map/ppermute | solution.py:302
  113.4 4.9 %collective-permute-start.37 = (f32[5,64]{1,0:T(8,128)S(1)}, f32[5,64]{1,0:T(8,128)S(1)}, u32[]{:S(2)}, u32[]{:S(2)}) collective-permute-start(f32[5,64]{1,0:T(8,128)S(1)} %get-tuple-element.82), channel_id=1, source_target_pairs={{0,30},{1,31},{2,0},{3,1},{4,2},{5,3},{6,4},{7,5},{8,6},{9,7},{10,... | collective-permute-start | bytes 3848 | tf_op jit(solution)/shard_map/ppermute | solution.py:302
  119.1 4.3 %fine_5.1 = f32[5,2048]{1,0:T(8,128)S(1)} custom-call(f32[5,2048]{1,0:T(8,128)S(1)} %get-tuple-element.78.x, f32[5,2048]{1,0:T(8,128)S(1)} %bitcast.66, f32[5,5,2048]{2,1,0:T(8,128)S(1)} %get-tuple-element.84.diag, f32[5,5,2048]{2,1,0:T(8,128)S(1)} %get-tuple-element.83.inverse, f32[6,5,5,2048]{3,2,1,0:T(8,128)S(1)} %bitcast.52, s32[6,2048]{1,0:T(8,128)S(1)} %bitcast.61, ...), custom_call_target="tpu_custom_call" | custom-call | tf_op jit(solution)/shard_map/fine_5/pallas_call | solution.py:289
  (110 shorter events, 25.6 us)
Async XLA Ops:
  2.9 11.5 %collective-permute-start = (f32[5,64]{1,0:T(8,128)S(1)}, f32[5,64]{1,0:T(8,128)S(1)}, u32[]{:S(2)}, u32[]{:S(2)}) collective-permute-start(f32[5,64]{1,0:T(8,128)S(1)} %get-tuple-element.44), channel_id=1, source_target_pairs={{0,2},{1,3},{2,4},{3,5},{4,6},{5,7},{6,8},{7,9},{8,10},{9,11},{10,... | collective-permute-start | bytes 3848 | tf_op jit(solution)/shard_map/ppermute | solution.py:302
  5.1 9.3 %collective-permute-start.1 = (f32[5,64]{1,0:T(8,128)S(1)}, f32[5,64]{1,0:T(8,128)S(1)}, u32[]{:S(2)}, u32[]{:S(2)}) collective-permute-start(f32[5,64]{1,0:T(8,128)S(1)} %get-tuple-element.45), channel_id=1, source_target_pairs={{0,1},{1,2},{2,3},{3,4},{4,5},{5,6},{6,7},{7,8},{8,9},{9,10},{10,1... | collective-permute-start | bytes 3848 | tf_op jit(solution)/shard_map/ppermute | solution.py:302
  7.2 7.2 %collective-permute-start.2 = (f32[5,64]{1,0:T(8,128)S(1)}, f32[5,64]{1,0:T(8,128)S(1)}, u32[]{:S(2)}, u32[]{:S(2)}) collective-permute-start(f32[5,64]{1,0:T(8,128)S(1)} %get-tuple-element.46), channel_id=1, source_target_pairs={{0,31},{1,0},{2,1},{3,2},{4,3},{5,4},{6,5},{7,6},{8,7},{9,8},{10,9... | collective-permute-start | bytes 3848 | tf_op jit(solution)/shard_map/ppermute | solution.py:302
  7.2 7.2 %collective-permute-start.3 = (f32[5,64]{1,0:T(8,128)S(1)}, f32[5,64]{1,0:T(8,128)S(1)}, u32[]{:S(2)}, u32[]{:S(2)}) collective-permute-start(f32[5,64]{1,0:T(8,128)S(1)} %get-tuple-element.47), channel_id=1, source_target_pairs={{0,30},{1,31},{2,0},{3,1},{4,2},{5,3},{6,4},{7,5},{8,6},{9,7},{10,... | collective-permute-start | bytes 3848 | tf_op jit(solution)/shard_map/ppermute | solution.py:302
  19.0 7.1 %collective-permute-start.4 = (f32[5,64]{1,0:T(8,128)S(1)}, f32[5,64]{1,0:T(8,128)S(1)}, u32[]{:S(2)}, u32[]{:S(2)}) collective-permute-start(f32[5,64]{1,0:T(8,128)S(1)} %get-tuple-element.49), channel_id=1, source_target_pairs={{0,2},{1,3},{2,4},{3,5},{4,6},{5,7},{6,8},{7,9},{8,10},{9,11},{10,... | collective-permute-start | bytes 3848 | tf_op jit(solution)/shard_map/ppermute | solution.py:302
  19.1 7.1 %collective-permute-start.5 = (f32[5,64]{1,0:T(8,128)S(1)}, f32[5,64]{1,0:T(8,128)S(1)}, u32[]{:S(2)}, u32[]{:S(2)}) collective-permute-start(f32[5,64]{1,0:T(8,128)S(1)} %get-tuple-element.50), channel_id=1, source_target_pairs={{0,1},{1,2},{2,3},{3,4},{4,5},{5,6},{6,7},{7,8},{8,9},{9,10},{10,1... | collective-permute-start | bytes 3848 | tf_op jit(solution)/shard_map/ppermute | solution.py:302
  31.5 8.0 %collective-permute-start.10 = (f32[5,64]{1,0:T(8,128)S(1)}, f32[5,64]{1,0:T(8,128)S(1)}, u32[]{:S(2)}, u32[]{:S(2)}) collective-permute-start(f32[5,64]{1,0:T(8,128)S(1)} %get-tuple-element.56), channel_id=1, source_target_pairs={{0,31},{1,0},{2,1},{3,2},{4,3},{5,4},{6,5},{7,6},{8,7},{9,8},{10,9... | collective-permute-start | bytes 3848 | tf_op jit(solution)/shard_map/ppermute | solution.py:302
  39.5 5.8 %collective-permute-start.8 = (f32[5,64]{1,0:T(8,128)S(1)}, f32[5,64]{1,0:T(8,128)S(1)}, u32[]{:S(2)}, u32[]{:S(2)}) collective-permute-start(f32[5,64]{1,0:T(8,128)S(1)} %get-tuple-element.54), channel_id=1, source_target_pairs={{0,2},{1,3},{2,4},{3,5},{4,6},{5,7},{6,8},{7,9},{8,10},{9,11},{10,... | collective-permute-start | bytes 3848 | tf_op jit(solution)/shard_map/ppermute | solution.py:302
  39.5 5.8 %collective-permute-start.9 = (f32[5,64]{1,0:T(8,128)S(1)}, f32[5,64]{1,0:T(8,128)S(1)}, u32[]{:S(2)}, u32[]{:S(2)}) collective-permute-start(f32[5,64]{1,0:T(8,128)S(1)} %get-tuple-element.55), channel_id=1, source_target_pairs={{0,1},{1,2},{2,3},{3,4},{4,5},{5,6},{6,7},{7,8},{8,9},{9,10},{10,1... | collective-permute-start | bytes 3848 | tf_op jit(solution)/shard_map/ppermute | solution.py:302
  53.3 7.4 %collective-permute-start.17 = (f32[5,512]{1,0:T(8,128)S(1)}, f32[5,512]{1,0:T(8,128)S(1)}, u32[]{:S(2)}, u32[]{:S(2)}) collective-permute-start(f32[5,512]{1,0:T(8,128)S(1)} %get-tuple-element.62.e), channel_id=1, source_target_pairs={{0,32},{32,0},{64,96},{96,64},{128,160},{160,128},{192,224},{224,1... | collective-permute-start | bytes 30728 | tf_op jit(solution)/shard_map/ppermute | solution.py:306
  54.4 6.1 %collective-permute-start.15 = (f32[5,32]{1,0:T(8,128)S(1)}, f32[5,32]{1,0:T(8,128)S(1)}, u32[]{:S(2)}, u32[]{:S(2)}) collective-permute-start(f32[5,32]{1,0:T(8,128)S(1)} %get-tuple-element.63), channel_id=1, source_target_pairs={{0,1},{1,2},{2,3},{3,4},{4,5},{5,6},{6,7},{7,8},{8,9},{9,10},{10,1... | collective-permute-start | bytes 1928 | tf_op jit(solution)/shard_map/ppermute | solution.py:302
  54.7 5.9 %collective-permute-start.16 = (f32[5,32]{1,0:T(8,128)S(1)}, f32[5,32]{1,0:T(8,128)S(1)}, u32[]{:S(2)}, u32[]{:S(2)}) collective-permute-start(f32[5,32]{1,0:T(8,128)S(1)} %get-tuple-element.64), channel_id=1, source_target_pairs={{0,31},{1,0},{2,1},{3,2},{4,3},{5,4},{6,5},{7,6},{8,7},{9,8},{10,9... | collective-permute-start | bytes 1928 | tf_op jit(solution)/shard_map/ppermute | solution.py:302
  74.2 10.0 %collective-permute-start.26 = (f32[5,512]{1,0:T(8,128)S(1)}, f32[5,512]{1,0:T(8,128)S(1)}, u32[]{:S(2)}, u32[]{:S(2)}) collective-permute-start(f32[5,512]{1,0:T(8,128)S(1)} %get-tuple-element.67.e), channel_id=1, source_target_pairs={{0,32},{32,0},{64,96},{96,64},{128,160},{160,128},{192,224},{224,1... | collective-permute-start | bytes 30728 | tf_op jit(solution)/shard_map/ppermute | solution.py:306
  74.2 9.7 %collective-permute-start.24 = (f32[5,32]{1,0:T(8,128)S(1)}, f32[5,32]{1,0:T(8,128)S(1)}, u32[]{:S(2)}, u32[]{:S(2)}) collective-permute-start(f32[5,32]{1,0:T(8,128)S(1)} %get-tuple-element.68), channel_id=1, source_target_pairs={{0,1},{1,2},{2,3},{3,4},{4,5},{5,6},{6,7},{7,8},{8,9},{9,10},{10,1... | collective-permute-start | bytes 1928 | tf_op jit(solution)/shard_map/ppermute | solution.py:302
  74.8 9.3 %collective-permute-start.25 = (f32[5,32]{1,0:T(8,128)S(1)}, f32[5,32]{1,0:T(8,128)S(1)}, u32[]{:S(2)}, u32[]{:S(2)}) collective-permute-start(f32[5,32]{1,0:T(8,128)S(1)} %get-tuple-element.69), channel_id=1, source_target_pairs={{0,31},{1,0},{2,1},{3,2},{4,3},{5,4},{6,5},{7,6},{8,7},{9,8},{10,9... | collective-permute-start | bytes 1928 | tf_op jit(solution)/shard_map/ppermute | solution.py:302
  84.6 8.3 %collective-permute-start.29 = (f32[5,512]{1,0:T(8,128)S(1)}, f32[5,512]{1,0:T(8,128)S(1)}, u32[]{:S(2)}, u32[]{:S(2)}) collective-permute-start(f32[5,512]{1,0:T(8,128)S(1)} %get-tuple-element.70.e), channel_id=1, source_target_pairs={{0,32},{32,0},{64,96},{96,64},{128,160},{160,128},{192,224},{224,1... | collective-permute-start | bytes 30728 | tf_op jit(solution)/shard_map/ppermute | solution.py:306
  86.3 6.5 %collective-permute-start.27 = (f32[5,32]{1,0:T(8,128)S(1)}, f32[5,32]{1,0:T(8,128)S(1)}, u32[]{:S(2)}, u32[]{:S(2)}) collective-permute-start(f32[5,32]{1,0:T(8,128)S(1)} %get-tuple-element.71), channel_id=1, source_target_pairs={{0,1},{1,2},{2,3},{3,4},{4,5},{5,6},{6,7},{7,8},{8,9},{9,10},{10,1... | collective-permute-start | bytes 1928 | tf_op jit(solution)/shard_map/ppermute | solution.py:302
  86.3 6.7 %collective-permute-start.28 = (f32[5,32]{1,0:T(8,128)S(1)}, f32[5,32]{1,0:T(8,128)S(1)}, u32[]{:S(2)}, u32[]{:S(2)}) collective-permute-start(f32[5,32]{1,0:T(8,128)S(1)} %get-tuple-element.72), channel_id=1, source_target_pairs={{0,31},{1,0},{2,1},{3,2},{4,3},{5,4},{6,5},{7,6},{8,7},{9,8},{10,9... | collective-permute-start | bytes 1928 | tf_op jit(solution)/shard_map/ppermute | solution.py:302
  94.3 11.2 %collective-permute-start.30 = (f32[5,64]{1,0:T(8,128)S(1)}, f32[5,64]{1,0:T(8,128)S(1)}, u32[]{:S(2)}, u32[]{:S(2)}) collective-permute-start(f32[5,64]{1,0:T(8,128)S(1)} %get-tuple-element.74), channel_id=1, source_target_pairs={{0,2},{1,3},{2,4},{3,5},{4,6},{5,7},{6,8},{7,9},{8,10},{9,11},{10,... | collective-permute-start | bytes 3848 | tf_op jit(solution)/shard_map/ppermute | solution.py:302
  94.3 11.2 %collective-permute-start.31 = (f32[5,64]{1,0:T(8,128)S(1)}, f32[5,64]{1,0:T(8,128)S(1)}, u32[]{:S(2)}, u32[]{:S(2)}) collective-permute-start(f32[5,64]{1,0:T(8,128)S(1)} %get-tuple-element.75), channel_id=1, source_target_pairs={{0,1},{1,2},{2,3},{3,4},{4,5},{5,6},{6,7},{7,8},{8,9},{9,10},{10,1... | collective-permute-start | bytes 3848 | tf_op jit(solution)/shard_map/ppermute | solution.py:302
  94.4 11.1 %collective-permute-start.32 = (f32[5,64]{1,0:T(8,128)S(1)}, f32[5,64]{1,0:T(8,128)S(1)}, u32[]{:S(2)}, u32[]{:S(2)}) collective-permute-start(f32[5,64]{1,0:T(8,128)S(1)} %get-tuple-element.76), channel_id=1, source_target_pairs={{0,31},{1,0},{2,1},{3,2},{4,3},{5,4},{6,5},{7,6},{8,7},{9,8},{10,9... | collective-permute-start | bytes 3848 | tf_op jit(solution)/shard_map/ppermute | solution.py:302
  100.0 5.8 %collective-permute-start.33 = (f32[5,64]{1,0:T(8,128)S(1)}, f32[5,64]{1,0:T(8,128)S(1)}, u32[]{:S(2)}, u32[]{:S(2)}) collective-permute-start(f32[5,64]{1,0:T(8,128)S(1)} %get-tuple-element.77), channel_id=1, source_target_pairs={{0,30},{1,31},{2,0},{3,1},{4,2},{5,3},{6,4},{7,5},{8,6},{9,7},{10,... | collective-permute-start | bytes 3848 | tf_op jit(solution)/shard_map/ppermute | solution.py:302
  110.4 8.0 %collective-permute-start.34 = (f32[5,64]{1,0:T(8,128)S(1)}, f32[5,64]{1,0:T(8,128)S(1)}, u32[]{:S(2)}, u32[]{:S(2)}) collective-permute-start(f32[5,64]{1,0:T(8,128)S(1)} %get-tuple-element.79), channel_id=1, source_target_pairs={{0,2},{1,3},{2,4},{3,5},{4,6},{5,7},{6,8},{7,9},{8,10},{9,11},{10,... | collective-permute-start | bytes 3848 | tf_op jit(solution)/shard_map/ppermute | solution.py:302
  110.4 7.9 %collective-permute-start.35 = (f32[5,64]{1,0:T(8,128)S(1)}, f32[5,64]{1,0:T(8,128)S(1)}, u32[]{:S(2)}, u32[]{:S(2)}) collective-permute-start(f32[5,64]{1,0:T(8,128)S(1)} %get-tuple-element.80), channel_id=1, source_target_pairs={{0,1},{1,2},{2,3},{3,4},{4,5},{5,6},{6,7},{7,8},{8,9},{9,10},{10,1... | collective-permute-start | bytes 3848 | tf_op jit(solution)/shard_map/ppermute | solution.py:302
  (30 other events, 271.6 us)
